TPU v7x, 256 devices: a whole 4x4x8 slice. The times are simulated.
256 devices in a mesh: clip: 64 (over x, z, core), slab: 4 (over y).
Axes of the slice: x: 4, y: 4, z: 8, core: 2. Of those that a mesh axis runs over, the one named last changes fastest.
Arguments:
- frames_in: bfloat16 [128, 16, 128, 128], P('clip', 'slab')
- clip_ids: int32 [64], replicated, may hold values from 0 to 15, never falling along the last dimension, each value on 1 to 32 neighbouring positions
- gain_one: float32 [128], replicated, may hold values from 0.25 to 1.75
- shift_one: float32 [128], replicated, may hold values from -3 to 3
- kernel_one: bfloat16 [3, 3, 3, 128, 128], replicated, may hold values from -0.109375 to 0.109375
- bias_one: float32 [128], replicated, may hold values from -3 to 3
- gain_two: float32 [128], replicated, may hold values from 0.25 to 1.75
- shift_two: float32 [128], replicated, may hold values from -3 to 3
- kernel_two: bfloat16 [3, 3, 3, 128, 128], replicated, may hold values from -0.109375 to 0.109375
- bias_two: float32 [128], replicated, may hold values from -3 to 3
Outputs:
- frames_out: bfloat16 [128, 16, 128, 128], P('clip', 'slab')
Inputs may be any that keep to these rules, and one draw needn't show every extreme that they name: `clip_ids`: never falling along the blocks; each clip covers 1 to 32 blocks, one exactly 32.
All inputs are finite; a program needn't handle non-finite values.
Results may differ from a plain program's by a relative error of at most 0.0075.
Values may be sent and summed in bfloat16 or wider, within the bound.
A program may use at most 64 MiB of HBM per device.

v0:
```python
import jax
import jax.numpy as jnp
from jax import lax
from jax.sharding import PartitionSpec as P

G = 32


def sent_to_all(array, axis):
    devices = lax.axis_size(axis)
    return lax.all_to_all(
        jnp.broadcast_to(array[None], (devices, *array.shape)), axis, 0, 0, tiled=True
    )


def of_everyone(array, axis):
    return sent_to_all(array, axis).sum(axis=0)


def joined_along(parts, dim):
    parts = jnp.moveaxis(parts, 0, dim)
    lengths = parts.shape
    return parts.reshape(*lengths[:dim], lengths[dim] * lengths[dim + 1], *lengths[dim + 2 :])


def collect(array, axis, dim):
    return joined_along(sent_to_all(array, axis), dim)


def from_behind(value, axis, steps):
    count = lax.axis_size(axis)
    leading, last = (max(0, -steps), min(count, count - steps))
    return lax.ppermute(value, axis, [(source, source + steps) for source in range(leading, last)])


def extended_2(cells, sides, width):
    for axis, dim in sides:
        count = lax.axis_size(axis)
        ends = count - 1
        head = lax.slice_in_dim(cells, 0, width, axis=dim)
        tail = lax.slice_in_dim(cells, cells.shape[dim] - width, cells.shape[dim], axis=dim)
        cells = jnp.concatenate(
            [
                lax.ppermute(tail, axis, [(i, (i + 1) % count) for i in range(ends)]),
                cells,
                lax.ppermute(head, axis, [((i + 1) % count, i) for i in range(ends)]),
            ],
            axis=dim,
        )
    return cells


def group_act(values, clip_ids, own_clip, gain, shift):
    floats = values.astype(jnp.float32)
    chan_count = values.shape[3]
    per_group = chan_count // G
    first = jnp.sum(floats, axis=(0, 1, 2)).reshape(G, per_group).sum(1)
    second = jnp.sum(floats * floats, axis=(0, 1, 2)).reshape(G, per_group).sum(1)
    local = jnp.stack([first, second], 0)
    slab_count = lax.axis_size("slab")
    match = (clip_ids == own_clip).astype(jnp.float32)
    summed = of_everyone(local, "slab")
    gathered = collect(summed[None], "clip", 0)
    totals = jnp.einsum("n,nkg->kg", match, gathered, precision=lax.Precision.HIGHEST)
    blocks = jnp.sum(match)
    counts = blocks * (values.shape[0] * values.shape[1] * slab_count * values.shape[2] * per_group)
    mean = totals[0] / counts
    spread = totals[1] / counts - mean * mean
    inverse = lax.rsqrt(spread + 1e-06)
    mean_chan = jnp.repeat(mean, per_group)
    inv_chan = jnp.repeat(inverse, per_group)
    normed = (floats - mean_chan) * inv_chan * gain + shift
    return jax.nn.silu(normed).astype(jnp.bfloat16)


def convolve(act, same_clip, kernel, bias):
    frame_count, row_count, col_count, chan_count = act.shape
    keep = same_clip.astype(jnp.bfloat16)
    carried = from_behind(act, "clip", 1) * keep
    extended = jnp.concatenate([carried, act], 0)
    padded = extended_2(extended, (("slab", 1),), 1)
    padded = jnp.pad(padded, ((0, 0), (0, 0), (1, 1), (0, 0)))
    total = jnp.zeros((frame_count * row_count * col_count, chan_count), jnp.float32)
    for time_off in range(3):
        for row_off in range(3):
            for col_off in range(3):
                window = padded[
                    time_off : time_off + frame_count,
                    row_off : row_off + row_count,
                    col_off : col_off + col_count,
                ].reshape(-1, chan_count)
                total = total + jnp.dot(
                    window, kernel[time_off, row_off, col_off], preferred_element_type=jnp.float32
                )
    return total.reshape(act.shape) + bias


def per_device(
    frames_in,
    clip_ids,
    gain_one,
    shift_one,
    kernel_one,
    bias_one,
    gain_two,
    shift_two,
    kernel_two,
    bias_two,
):
    position = lax.axis_index("clip")
    own_clip = lax.dynamic_index_in_dim(clip_ids, position, 0, keepdims=False)
    prior_clip = lax.dynamic_index_in_dim(clip_ids, jnp.maximum(position - 1, 0), 0, keepdims=False)
    same_clip = jnp.logical_and(position > 0, prior_clip == own_clip)
    act_one = group_act(frames_in, clip_ids, own_clip, gain_one, shift_one)
    hidden = convolve(act_one, same_clip, kernel_one, bias_one).astype(jnp.bfloat16)
    act_two = group_act(hidden, clip_ids, own_clip, gain_two, shift_two)
    branch = convolve(act_two, same_clip, kernel_two, bias_two)
    return (frames_in.astype(jnp.float32) + branch).astype(jnp.bfloat16)


def solution(mesh):
    placed = (P("clip", "slab", None, None), P(), P(), P(), P(), P(), P(), P(), P(), P())
    return jax.shard_map(
        per_device,
        mesh=mesh,
        in_specs=placed,
        out_specs=P("clip", "slab", None, None),
        check_vma=False,
    )
```

profile of v0, /device:TPU:2, one launch (start us, length us, event | category | flops | bytes accessed | tf_op | source)
XLA Modules:
  0.0 115.3 jit_solution(15140697998865031838)
XLA Ops:
  0.0 1.2 %convert_reduce_fusion = (f32[128]{0:T(128)S(1)}, f32[128]{0:T(128)S(1)}) fusion(bf16[2,4,128,128]{3,2,1,0:T(8,128)(2,1)} %param.10), kind=kLoop, calls=%fused_computation.58 | loop fusion | flops 524032 | bytes 263168 | tf_op jit(solution)/shard_map/reduce_sum | solution.py:57
  2.2 4.5 %all-to-all-start = ((f32[4,2,32]{2,1,0:T(2,128)}), f32[4,2,32]{2,1,0:T(2,128)S(1)}, u32[]{:S(2)}, u32[]{:S(2)}) async-start(f32[4,2,32]{2,1,0:T(2,128)} %broadcast_in_dim.16), calls=%async_computation | async-start | bytes 8192 | tf_op jit(solution)/shard_map/all_to_all | solution.py:11
  6.7 1.4 %fusion.169 = (s32[1]{0:T(128)}, s32[1]{0:T(128)}) fusion(s32[64]{0:T(128)} %param.11, s32[]{:T(128)S(6)} %max.3, s32[]{:T(128)S(6)} %select_n.5), kind=kLoop, calls=%fused_computation.252 | loop fusion | bytes 24 | tf_op jit(solution)/shard_map/jit(dynamic_index_in_dim)/dynamic_slice | solution.py:112
  8.1 3.9 %all-to-all-done = f32[4,2,32]{2,1,0:T(2,128)S(1)} async-done(((f32[4,2,32]{2,1,0:T(2,128)}), f32[4,2,32]{2,1,0:T(2,128)S(1)}, u32[]{:S(2)}, u32[]{:S(2)}) %all-to-all-start) | async-done | bytes 1056 | tf_op jit(solution)/shard_map/all_to_all | solution.py:11
  12.7 12.0 %all-to-all-start.1 = ((f32[64,1,2,32]{3,2,1,0:T(2,128)}), f32[64,1,2,32]{3,2,1,0:T(2,128)S(1)}, u32[]{:S(2)}, u32[]{:S(2)}) async-start(f32[64,1,2,32]{3,2,1,0:T(2,128)} %broadcast_in_dim.17), calls=%async_computation.1 | async-start | bytes 131072 | tf_op jit(solution)/shard_map/all_to_all | solution.py:11
  24.7 1.8 %convert_reduce_fusion.2 = f32[]{:T(128)} fusion(s32[64]{0:T(128)} %param.11, s32[]{:T(128)} %bitcast), kind=kLoop, calls=%fused_computation.243 | loop fusion | flops 191 | bytes 264 | tf_op jit(solution)/shard_map/reduce_sum | solution.py:65
  27.2 6.3 %all-to-all-done.1 = f32[64,1,2,32]{3,2,1,0:T(2,128)S(1)} async-done(((f32[64,1,2,32]{3,2,1,0:T(2,128)}), f32[64,1,2,32]{3,2,1,0:T(2,128)S(1)}, u32[]{:S(2)}, u32[]{:S(2)}) %all-to-all-start.1) | async-done | bytes 16416 | tf_op jit(solution)/shard_map/all_to_all | solution.py:11
  33.5 1.3 %fusion.42 = f32[1,2,32]{2,0,1:T(1,128)S(1)} fusion(f32[64,2,32]{2,1,0:T(2,128)S(1)} %bitcast.363, s32[64]{0:T(128)} %param.11, s32[]{:T(128)} %bitcast), kind=kOutput, calls=%fused_computation.117 | convolution fusion | flops 49216 | bytes 16900 | tf_op jit(solution)/shard_map/n,nkg->kg/dot_general | solution.py:64
  36.1 2.0 %collective-permute-start = (bf16[2,4,128,128]{3,2,1,0:T(8,128)(2,1)S(1)}, bf16[2,4,128,128]{3,2,1,0:T(8,128)(2,1)S(1)}, u32[]{:S(2)}, u32[]{:S(2)}) collective-permute-start(bf16[2,4,128,128]{3,2,1,0:T(8,128)(2,1)S(1)} %fusion.32), channel_id=1, source_target_pairs={{0,4},{4,8},{8,12},{12,16},{16,20},{20,24},{24,28},{28,32},{32,36}... | collective-permute-start | bytes 786440 | tf_op jit(solution)/shard_map/ppermute | solution.py:33
  39.4 6.5 %collective-permute-done = bf16[2,4,128,128]{3,2,1,0:T(8,128)(2,1)S(1)} collective-permute-done((bf16[2,4,128,128]{3,2,1,0:T(8,128)(2,1)S(1)}, bf16[2,4,128,128]{3,2,1,0:T(8,128)(2,1)S(1)}, u32[]{:S(2)}, u32[]{:S(2)}) %collective-permute-start) | collective-permute-done | bytes 262176 | tf_op jit(solution)/shard_map/ppermute | solution.py:33
  46.0 2.5 %collective-permute-start.1 = (bf16[4,1,128,128]{3,2,1,0:T(8,128)(2,1)S(1)}, bf16[4,1,128,128]{3,2,1,0:T(8,128)(2,1)S(1)}, u32[]{:S(2)}, u32[]{:S(2)}) collective-permute-start(bf16[4,1,128,128]{3,2,1,0:T(8,128)(2,1)S(1)} %get-tuple-element.68), channel_id=1, source_target_pairs={{0,1},{1,2},{2,3},{4,5},{5,6},{6,7},{8,9},{9,10},{10,11},{12,13},{... | collective-permute-start | bytes 393224 | tf_op jit(solution)/shard_map/ppermute | solution.py:44
  48.5 1.3 %collective-permute-start.2 = (bf16[4,1,128,128]{3,2,1,0:T(8,128)(2,1)S(1)}, bf16[4,1,128,128]{3,2,1,0:T(8,128)(2,1)S(1)}, u32[]{:S(2)}, u32[]{:S(2)}) collective-permute-start(bf16[4,1,128,128]{3,2,1,0:T(8,128)(2,1)S(1)} %get-tuple-element.69), channel_id=1, source_target_pairs={{1,0},{2,1},{3,2},{5,4},{6,5},{7,6},{9,8},{10,9},{11,10},{13,12},{... | collective-permute-start | bytes 393224 | tf_op jit(solution)/shard_map/ppermute | solution.py:46
  49.8 1.2 %collective-permute-done.1 = bf16[4,1,128,128]{3,2,1,0:T(8,128)(2,1)S(1)} collective-permute-done((bf16[4,1,128,128]{3,2,1,0:T(8,128)(2,1)S(1)}, bf16[4,1,128,128]{3,2,1,0:T(8,128)(2,1)S(1)}, u32[]{:S(2)}, u32[]{:S(2)}) %collective-permute-start.1) | collective-permute-done | bytes 131104 | tf_op jit(solution)/shard_map/ppermute | solution.py:44
  51.0 4.4 %collective-permute-done.2 = bf16[4,1,128,128]{3,2,1,0:T(8,128)(2,1)S(1)} collective-permute-done((bf16[4,1,128,128]{3,2,1,0:T(8,128)(2,1)S(1)}, bf16[4,1,128,128]{3,2,1,0:T(8,128)(2,1)S(1)}, u32[]{:S(2)}, u32[]{:S(2)}) %collective-permute-start.2) | collective-permute-done | bytes 131104 | tf_op jit(solution)/shard_map/ppermute | solution.py:46
  55.6 0.9 fusion.164
  64.0 8.5 %all_to_all.20 = f32[4,2,32]{2,1,0:T(2,128)S(1)} all-to-all(f32[4,2,32]{2,1,0:T(2,128)S(1)} %broadcast_in_dim.20), channel_id=1, replica_groups=mesh['clip'=64,'slab'=4] {'slab'}, dimensions={0} | all-to-all | bytes 2048 | tf_op jit(solution)/shard_map/all_to_all | solution.py:11
  72.6 13.3 %all_to_all.21 = f32[64,1,2,32]{3,2,1,0:T(2,128)S(1)} all-to-all(f32[64,1,2,32]{3,2,1,0:T(2,128)S(1)} %broadcast_in_dim.21), channel_id=1, replica_groups=mesh['clip'=64,'slab'=4] {'clip'}, dimensions={0} | all-to-all | bytes 32768 | tf_op jit(solution)/shard_map/all_to_all | solution.py:11
  87.1 2.0 %collective-permute-start.3 = (bf16[2,4,128,128]{3,2,1,0:T(8,128)(2,1)S(1)}, bf16[2,4,128,128]{3,2,1,0:T(8,128)(2,1)S(1)}, u32[]{:S(2)}, u32[]{:S(2)}) collective-permute-start(bf16[2,4,128,128]{3,2,1,0:T(8,128)(2,1)S(1)} %multiply_convert_fusion), channel_id=1, source_target_pairs={{0,4},{4,8},{8,12},{12,16},{16,20},{20,24},{24,28},{28,32},{32,36}... | collective-permute-start | bytes 786440 | tf_op jit(solution)/shard_map/ppermute | solution.py:33
  89.2 7.8 %collective-permute-done.3 = bf16[2,4,128,128]{3,2,1,0:T(8,128)(2,1)S(1)} collective-permute-done((bf16[2,4,128,128]{3,2,1,0:T(8,128)(2,1)S(1)}, bf16[2,4,128,128]{3,2,1,0:T(8,128)(2,1)S(1)}, u32[]{:S(2)}, u32[]{:S(2)}) %collective-permute-start.3) | collective-permute-done | bytes 262176 | tf_op jit(solution)/shard_map/ppermute | solution.py:33
  97.0 2.5 %collective-permute-start.4 = (bf16[4,1,128,128]{3,2,1,0:T(8,128)(2,1)S(1)}, bf16[4,1,128,128]{3,2,1,0:T(8,128)(2,1)S(1)}, u32[]{:S(2)}, u32[]{:S(2)}) collective-permute-start(bf16[4,1,128,128]{3,2,1,0:T(8,128)(2,1)S(1)} %get-tuple-element.64), channel_id=1, source_target_pairs={{0,1},{1,2},{2,3},{4,5},{5,6},{6,7},{8,9},{9,10},{10,11},{12,13},{... | collective-permute-start | bytes 393224 | tf_op jit(solution)/shard_map/ppermute | solution.py:44
  99.5 1.5 %collective-permute-start.5 = (bf16[4,1,128,128]{3,2,1,0:T(8,128)(2,1)S(1)}, bf16[4,1,128,128]{3,2,1,0:T(8,128)(2,1)S(1)}, u32[]{:S(2)}, u32[]{:S(2)}) collective-permute-start(bf16[4,1,128,128]{3,2,1,0:T(8,128)(2,1)S(1)} %get-tuple-element.65), channel_id=1, source_target_pairs={{1,0},{2,1},{3,2},{5,4},{6,5},{7,6},{9,8},{10,9},{11,10},{13,12},{... | collective-permute-start | bytes 393224 | tf_op jit(solution)/shard_map/ppermute | solution.py:46
  101.0 1.0 collective-permute-done.4
  102.0 4.4 %collective-permute-done.5 = bf16[4,1,128,128]{3,2,1,0:T(8,128)(2,1)S(1)} collective-permute-done((bf16[4,1,128,128]{3,2,1,0:T(8,128)(2,1)S(1)}, bf16[4,1,128,128]{3,2,1,0:T(8,128)(2,1)S(1)}, u32[]{:S(2)}, u32[]{:S(2)}) %collective-permute-start.5) | collective-permute-done | bytes 131104 | tf_op jit(solution)/shard_map/ppermute | solution.py:46
  106.8 0.9 fusion.163
  (113 shorter events, 19.8 us)
Async XLA Ops:
  0.0 35.3 %copy-start = (bf16[2,4,128,128]{3,2,1,0:T(8,128)(2,1)S(1)}, bf16[2,4,128,128]{3,2,1,0:T(8,128)(2,1)}, u32[]{:S(2)}) copy-start(bf16[2,4,128,128]{3,2,1,0:T(8,128)(2,1)} %param.10) | copy-start | bytes 786436
  2.2 9.8 %all-to-all-start = ((f32[4,2,32]{2,1,0:T(2,128)}), f32[4,2,32]{2,1,0:T(2,128)S(1)}, u32[]{:S(2)}, u32[]{:S(2)}) async-start(f32[4,2,32]{2,1,0:T(2,128)} %broadcast_in_dim.16), calls=%async_computation | async-start | bytes 8192 | tf_op jit(solution)/shard_map/all_to_all | solution.py:11
  12.7 20.9 %all-to-all-start.1 = ((f32[64,1,2,32]{3,2,1,0:T(2,128)}), f32[64,1,2,32]{3,2,1,0:T(2,128)S(1)}, u32[]{:S(2)}, u32[]{:S(2)}) async-start(f32[64,1,2,32]{3,2,1,0:T(2,128)} %broadcast_in_dim.17), calls=%async_computation.1 | async-start | bytes 131072 | tf_op jit(solution)/shard_map/all_to_all | solution.py:11
  36.1 9.8 %collective-permute-start = (bf16[2,4,128,128]{3,2,1,0:T(8,128)(2,1)S(1)}, bf16[2,4,128,128]{3,2,1,0:T(8,128)(2,1)S(1)}, u32[]{:S(2)}, u32[]{:S(2)}) collective-permute-start(bf16[2,4,128,128]{3,2,1,0:T(8,128)(2,1)S(1)} %fusion.32), channel_id=1, source_target_pairs={{0,4},{4,8},{8,12},{12,16},{16,20},{20,24},{24,28},{28,32},{32,36}... | collective-permute-start | bytes 786440 | tf_op jit(solution)/shard_map/ppermute | solution.py:33
  46.0 5.0 %collective-permute-start.1 = (bf16[4,1,128,128]{3,2,1,0:T(8,128)(2,1)S(1)}, bf16[4,1,128,128]{3,2,1,0:T(8,128)(2,1)S(1)}, u32[]{:S(2)}, u32[]{:S(2)}) collective-permute-start(bf16[4,1,128,128]{3,2,1,0:T(8,128)(2,1)S(1)} %get-tuple-element.68), channel_id=1, source_target_pairs={{0,1},{1,2},{2,3},{4,5},{5,6},{6,7},{8,9},{9,10},{10,11},{12,13},{... | collective-permute-start | bytes 393224 | tf_op jit(solution)/shard_map/ppermute | solution.py:44
  48.5 6.9 %collective-permute-start.2 = (bf16[4,1,128,128]{3,2,1,0:T(8,128)(2,1)S(1)}, bf16[4,1,128,128]{3,2,1,0:T(8,128)(2,1)S(1)}, u32[]{:S(2)}, u32[]{:S(2)}) collective-permute-start(bf16[4,1,128,128]{3,2,1,0:T(8,128)(2,1)S(1)} %get-tuple-element.69), channel_id=1, source_target_pairs={{1,0},{2,1},{3,2},{5,4},{6,5},{7,6},{9,8},{10,9},{11,10},{13,12},{... | collective-permute-start | bytes 393224 | tf_op jit(solution)/shard_map/ppermute | solution.py:46
  55.6 1.2 %copy-start.1 = (bf16[3,3,3,128,128]{4,3,2,1,0:T(8,128)(2,1)S(1)}, bf16[3,3,3,128,128]{4,3,2,1,0:T(8,128)(2,1)}, u32[]{:S(2)}) copy-start(bf16[3,3,3,128,128]{4,3,2,1,0:T(8,128)(2,1)} %param.14) | copy-start | bytes 2654212
  62.6 0.7 copy-start.4
  63.2 22.6 %copy-start.3 = (s32[64]{0:T(128)S(1)}, s32[64]{0:T(128)}, u32[]{:S(2)}) copy-start(s32[64]{0:T(128)} %param.11) | copy-start | bytes 772
  63.3 23.7 %copy-start.6 = (f32[128]{0:T(128)S(1)}, f32[128]{0:T(128)}, u32[]{:S(2)}) copy-start(f32[128]{0:T(128)} %param.17) | copy-start | bytes 1540
  63.3 23.7 %copy-start.7 = (f32[128]{0:T(128)S(1)}, f32[128]{0:T(128)}, u32[]{:S(2)}) copy-start(f32[128]{0:T(128)} %param.16) | copy-start | bytes 1540
  87.1 9.8 %collective-permute-start.3 = (bf16[2,4,128,128]{3,2,1,0:T(8,128)(2,1)S(1)}, bf16[2,4,128,128]{3,2,1,0:T(8,128)(2,1)S(1)}, u32[]{:S(2)}, u32[]{:S(2)}) collective-permute-start(bf16[2,4,128,128]{3,2,1,0:T(8,128)(2,1)S(1)} %multiply_convert_fusion), channel_id=1, source_target_pairs={{0,4},{4,8},{8,12},{12,16},{16,20},{20,24},{24,28},{28,32},{32,36}... | collective-permute-start | bytes 786440 | tf_op jit(solution)/shard_map/ppermute | solution.py:33
  97.0 5.0 %collective-permute-start.4 = (bf16[4,1,128,128]{3,2,1,0:T(8,128)(2,1)S(1)}, bf16[4,1,128,128]{3,2,1,0:T(8,128)(2,1)S(1)}, u32[]{:S(2)}, u32[]{:S(2)}) collective-permute-start(bf16[4,1,128,128]{3,2,1,0:T(8,128)(2,1)S(1)} %get-tuple-element.64), channel_id=1, source_target_pairs={{0,1},{1,2},{2,3},{4,5},{5,6},{6,7},{8,9},{9,10},{10,11},{12,13},{... | collective-permute-start | bytes 393224 | tf_op jit(solution)/shard_map/ppermute | solution.py:44
  99.5 6.9 %collective-permute-start.5 = (bf16[4,1,128,128]{3,2,1,0:T(8,128)(2,1)S(1)}, bf16[4,1,128,128]{3,2,1,0:T(8,128)(2,1)S(1)}, u32[]{:S(2)}, u32[]{:S(2)}) collective-permute-start(bf16[4,1,128,128]{3,2,1,0:T(8,128)(2,1)S(1)} %get-tuple-element.65), channel_id=1, source_target_pairs={{1,0},{2,1},{3,2},{5,4},{6,5},{7,6},{9,8},{10,9},{11,10},{13,12},{... | collective-permute-start | bytes 393224 | tf_op jit(solution)/shard_map/ppermute | solution.py:46
  106.8 1.2 %copy-start.2 = (bf16[3,3,3,128,128]{4,3,2,1,0:T(8,128)(2,1)S(1)}, bf16[3,3,3,128,128]{4,3,2,1,0:T(8,128)(2,1)}, u32[]{:S(2)}) copy-start(bf16[3,3,3,128,128]{4,3,2,1,0:T(8,128)(2,1)} %param.18) | copy-start | bytes 2654212
  113.9 0.7 copy-start.5
where the time goes:
time: 116 us; the launch traced here: 115 us
  waiting for transfers between devices  35.4 us (31%)
  starting transfers between devices  28.3 us (24%)
  blocking collectives  21.7 us (19%)
  matrix products  13.6 us (12%)
  local copies, waits for them, and re-layouts  7.55 us (7%)
  other arithmetic  6.25 us (5%)
  between operations  2.53 us (2%)
    all_to_all x2, blocking collectives, sent_to_all(): lax.all_to_all(jnp.broadcast_to(array[None], (devices, *array.shape)), ax...  21.7 us
    all_to_all x2, starting transfers between devices, sent_to_all(): lax.all_to_all(jnp.broadcast_to(array[None], (devices, *array.shape)), ax...  16.5 us
    ppermute x2, waiting for transfers between devices, from_behind(): lax.ppermute(value, axis, [(source, source + steps) for source in range(l...  14.3 us
    dot_general x54, matrix products, convolve(): jnp.dot(window, kernel[time_off, row_off, col_off], preferred_element_typ...  11.6 us
    all_to_all x2, waiting for transfers between devices, sent_to_all(): lax.all_to_all(jnp.broadcast_to(array[None], (devices, *array.shape)), ax...  10.2 us
    ppermute x2, waiting for transfers between devices, extended_2(): lax.ppermute(head, axis, [((i + 1) % count, i) for i in range(ends)])  8.73 us
    ppermute x2, starting transfers between devices, extended_2(): lax.ppermute(tail, axis, [(i, (i + 1) % count) for i in range(ends)])  4.95 us
    ppermute x2, starting transfers between devices, from_behind(): lax.ppermute(value, axis, [(source, source + steps) for source in range(l...  4.05 us
  transfers between devices with their start and end apart: 8, of which 8 were waited for; matrix products, arithmetic and copies ran while one was open for 3% of the time, Pallas kernels for 0%

commit v1 on v0

v1 whole, which is shorter than its diff:
```python
import functools

import jax
import jax.numpy as jnp
from jax import lax
from jax.experimental import pallas as pl
from jax.experimental.pallas import tpu as pltpu
from jax.sharding import PartitionSpec as P

MESH = pl.DeviceIdType.MESH
NX, NZ, NC, NY = 4, 8, 2, 4
CH = 128
W = 128
EPS = 1e-06


def hops(dx, dz, dy):
    return min(dx, NX - dx) + min(dz, NZ - dz) + min(dy, NY - dy)


NEAR = sorted(
    [(dy, dc) for dy in range(NY) for dc in range(NC) if dy or dc],
    key=lambda o: -hops(0, 0, o[0]),
)
FAR = sorted(
    [(dx, dz) for dx in range(NX) for dz in range(NZ) if dx or dz],
    key=lambda o: -hops(o[0], o[1], 0),
)


def kernel(
    x_hbm, ids_hbm, g1, s1, k1, b1, g2, s2, k2, b2, out_ref,
    xbuf, hbuf, act, wts, pbuf, ids, vecs, near, far, mask,
    load_sem, w_sem, halo_send, halo_recv, st_send, st_recv,
):
    clip = lax.axis_index("clip")
    y = lax.axis_index("slab")
    cx = clip // (NZ * NC)
    cz = (clip // NC) % NZ
    cc = clip % NC
    clips = NX * NZ * NC

    def near_dev(o):
        return (clip - cc + (cc + o[1]) % NC, (y + o[0]) % NY)

    def far_dev(o):
        return (((cx + o[0]) % NX) * (NZ * NC) + ((cz + o[1]) % NZ) * NC + cc, y)

    nxt, prv = (clip + 1) % clips, (clip + clips - 1) % clips
    up, down = (y + 1) % NY, (y + NY - 1) % NY
    halo_peers = [(nxt, y), (nxt, up), (nxt, down), (prv, y), (prv, up), (prv, down)]

    barrier = pltpu.get_barrier_semaphore()
    n_signals = 0
    for dev in [far_dev(o) for o in FAR] + halo_peers + [near_dev(o) for o in NEAR]:
        pl.semaphore_signal(barrier, inc=1, device_id=dev, device_id_type=MESH)
        n_signals += 1

    loads = [pltpu.make_async_copy(x_hbm, xbuf.at[pl.ds(2, 2), pl.ds(1, 4)], load_sem.at[0])]
    loads.append(pltpu.make_async_copy(ids_hbm, ids, load_sem.at[1]))
    for n, v in enumerate((g1, s1, b1, g2, s2, b2)):
        loads.append(pltpu.make_async_copy(v, vecs.at[n], load_sem.at[2 + n]))
    for cp in loads:
        cp.start()
    w_loads = []
    for cv, k in enumerate((k1, k2)):
        for dt in range(3):
            for dx in range(3):
                for i in range(2):
                    j = dt + i
                    cp = pltpu.make_async_copy(
                        k.at[dt, :, dx],
                        wts.at[cv, dx, :, pl.ds(j * CH, CH), pl.ds(i * CH, CH)],
                        w_sem.at[cv, len(w_loads) % 18],
                    )
                    cp.start()
                    w_loads.append(cp)

    def stats_of(rows):
        s = jnp.zeros((8, CH), jnp.float32)
        q = jnp.zeros((8, CH), jnp.float32)
        for v in rows:
            v = v.reshape(W // 8, 8, CH)
            s = s + jnp.sum(v, axis=0)
            q = q + jnp.sum(v * v, axis=0)
        return s, q

    def packed(s, q):
        return jnp.concatenate(
            [jnp.sum(s, axis=0, keepdims=True), jnp.sum(q, axis=0, keepdims=True)], axis=0
        )

    loads[0].wait()
    s, q = stats_of(
        xbuf[2 + f, 1 + r].astype(jnp.float32) for f in range(2) for r in range(4)
    )
    me_near = y * NC + cc
    me_far = cx * NZ + cz
    near[0, me_near] = packed(s, q)

    pl.semaphore_wait(barrier, n_signals)

    def near_sends(ar):
        cps = []
        for o in NEAR:
            cp = pltpu.make_async_remote_copy(
                src_ref=near.at[ar, me_near], dst_ref=near.at[ar, me_near],
                send_sem=st_send.at[ar, 0], recv_sem=st_recv.at[ar, 0],
                device_id=near_dev(o), device_id_type=MESH,
            )
            cp.start()
            cps.append(cp)
        return cps

    def far_sends(ar):
        cps = []
        for o in FAR:
            cp = pltpu.make_async_remote_copy(
                src_ref=far.at[ar, me_far], dst_ref=far.at[ar, me_far],
                send_sem=st_send.at[ar, 1], recv_sem=st_recv.at[ar, 1],
                device_id=far_dev(o), device_id_type=MESH,
            )
            cp.start()
            cps.append(cp)
        return cps

    def halo_sends(buf, n):
        own = buf.at[pl.ds(2, 2), pl.ds(1, 4)]
        first = buf.at[pl.ds(2, 2), 1]
        last = buf.at[pl.ds(2, 2), 4]
        plan = [
            (own, buf.at[pl.ds(0, 2), pl.ds(1, 4)], (nxt, y)),
            (last, buf.at[pl.ds(0, 2), 0], (nxt, up)),
            (first, buf.at[pl.ds(0, 2), 5], (nxt, down)),
            (last, buf.at[pl.ds(2, 2), 0], (clip, up)),
            (first, buf.at[pl.ds(2, 2), 5], (clip, down)),
        ]
        cps = []
        for m, (src, dst, dev) in enumerate(plan):
            cp = pltpu.make_async_remote_copy(
                src_ref=src, dst_ref=dst, send_sem=halo_send.at[n, m],
                recv_sem=halo_recv.at[n, m], device_id=dev, device_id_type=MESH,
            )
            cp.start()
            cps.append(cp)
        return cps

    def wait_near(ar):
        got = near.at[ar, pl.ds(0, len(NEAR))]
        pltpu.make_async_copy(got, got, st_recv.at[ar, 0]).wait()

    def wait_far(ar):
        got = far.at[ar, pl.ds(0, len(FAR))]
        pltpu.make_async_copy(got, got, st_recv.at[ar, 1]).wait()

    def fold(ar):
        for c in range(NC):
            t = near[ar, c]
            for k in range(1, NY):
                t = t + near[ar, k * NC + c]
            far[ar, me_far, 2 * c : 2 * c + 2, :] = t

    near_1 = near_sends(0)
    halo_1 = halo_sends(xbuf, 0)

    for cp in loads[1:]:
        cp.wait()
    own_id = ids[clip]
    blocks = jnp.float32(0)
    for k in range(NX * NZ):
        for c in range(NC):
            m = jnp.where(ids[k * NC + c] == own_id, jnp.float32(1), jnp.float32(0))
            blocks = blocks + m
            mask[k, 2 * c : 2 * c + 2, :] = jnp.full((2, CH), m, jnp.float32)
    prior_id = ids[jnp.maximum(clip - 1, 0)]
    same = jnp.where(prior_id == own_id, jnp.float32(1), jnp.float32(0))
    same = same * jnp.where(clip > 0, jnp.float32(1), jnp.float32(0))
    top = jnp.where(y > 0, jnp.float32(1), jnp.float32(0))
    bottom = jnp.where(y < NY - 1, jnp.float32(1), jnp.float32(0))
    one_count = 1.0 / (jnp.full((1, CH), blocks, jnp.float32) * (2 * 4 * NY * W * 4))
    zero = jnp.zeros((CH, CH), jnp.bfloat16)
    for cv in range(2):
        for dx in range(3):
            for dy in range(3):
                wts[cv, dx, dy, 0:CH, CH : 2 * CH] = zero
                wts[cv, dx, dy, 3 * CH : 4 * CH, 0:CH] = zero
    lane = lax.broadcasted_iota(jnp.int32, (2, CH), 1)

    def finish(ar, gain, shift):
        acc = jnp.zeros((4, CH), jnp.float32)
        for k in range(NX * NZ):
            acc = acc + far[ar, k] * mask[k]
        t = acc[0:2] + acc[2:4]
        t = t + jnp.where(lane % 2 == 0, pltpu.roll(t, CH - 1, 1), pltpu.roll(t, 1, 1))
        t = t + jnp.where(lane % 4 < 2, pltpu.roll(t, CH - 2, 1), pltpu.roll(t, 2, 1))
        mean = t[0:1] * one_count
        spread = t[1:2] * one_count - mean * mean
        inverse = lax.rsqrt(spread + EPS)
        scale = inverse * gain
        return 0.5 * scale, 0.5 * (shift - mean * scale)

    def activate(buf, scale, offset):
        for r in range(6):
            row = top if r == 0 else bottom if r == 5 else None
            for j in range(4):
                keep = row
                if j < 2:
                    keep = same if row is None else same * row
                sc, of = (scale, offset) if keep is None else (scale * keep, offset * keep)
                h = buf[j, r].astype(jnp.float32) * sc + of
                v = h + h * jnp.tanh(h)
                act[r * W : (r + 1) * W, j * CH : (j + 1) * CH] = v.astype(jnp.bfloat16)

    def convolve(cv):
        lhs = jnp.concatenate([act[d * W : (d + 4) * W, :] for d in range(3)], axis=1)
        for dx in range(3):
            rhs = wts[cv, dx].reshape(3 * 4 * CH, 2 * CH)
            pbuf[dx] = jnp.dot(lhs, rhs, preferred_element_type=jnp.float32)

    col = lax.broadcasted_iota(jnp.int32, (W, CH), 0)

    def joined(f, r, bias):
        at = (slice(r * W, (r + 1) * W), slice(f * CH, (f + 1) * CH))
        left = jnp.where(col == 0, 0.0, pltpu.roll(pbuf[(0, *at)], 1, 0))
        right = jnp.where(col == W - 1, 0.0, pltpu.roll(pbuf[(2, *at)], W - 1, 0))
        return (left + pbuf[(1, *at)]) + (right + bias)

    wait_near(0)
    fold(0)
    far_1 = far_sends(0)
    for cp in w_loads:
        cp.wait()
    for cp in halo_1:
        cp.wait_recv()
    wait_far(0)
    scale, offset = finish(0, vecs[0], vecs[1])
    activate(xbuf, scale, offset)
    convolve(0)

    def hidden_rows():
        for f in range(2):
            for r in range(4):
                v = joined(f, r, vecs[2]).astype(jnp.bfloat16)
                hbuf[2 + f, 1 + r] = v
                yield v.astype(jnp.float32)

    s, q = stats_of(hidden_rows())
    near[1, me_near] = packed(s, q)
    near_2 = near_sends(1)
    halo_2 = halo_sends(hbuf, 1)
    wait_near(1)
    fold(1)
    far_2 = far_sends(1)
    for cp in halo_2:
        cp.wait_recv()
    wait_far(1)
    scale, offset = finish(1, vecs[3], vecs[4])
    activate(hbuf, scale, offset)
    convolve(1)
    for f in range(2):
        for r in range(4):
            v = joined(f, r, vecs[5]) + xbuf[2 + f, 1 + r].astype(jnp.float32)
            out_ref[f, r] = v.astype(jnp.bfloat16)
    for cp in near_1 + near_2 + far_1 + far_2 + halo_1 + halo_2:
        cp.wait_send()


def per_device(x, ids, g1, s1, k1, b1, g2, s2, k2, b2):
    vec = [v.reshape(1, CH) for v in (g1, s1, b1, g2, s2, b2)]
    g1, s1, b1, g2, s2, b2 = vec
    anywhere = pl.BlockSpec(memory_space=pl.ANY)
    operands = [
        pltpu.with_memory_space_constraint(v, pltpu.HBM)
        for v in (x, ids, g1, s1, k1, b1, g2, s2, k2, b2)
    ]
    bf16, f32 = jnp.bfloat16, jnp.float32
    return pl.pallas_call(
        kernel,
        out_shape=jax.ShapeDtypeStruct(x.shape, bf16),
        in_specs=[anywhere] * 10,
        out_specs=pl.BlockSpec(memory_space=pltpu.VMEM),
        scratch_shapes=[
            pltpu.VMEM((4, 6, W, CH), bf16),
            pltpu.VMEM((4, 6, W, CH), bf16),
            pltpu.VMEM((6 * W, 4 * CH), bf16),
            pltpu.VMEM((2, 3, 3, 4 * CH, 2 * CH), bf16),
            pltpu.VMEM((3, 4 * W, 2 * CH), f32),
            pltpu.SMEM((64,), jnp.int32),
            pltpu.VMEM((6, 1, CH), f32),
            pltpu.VMEM((2, NY * NC, 2, CH), f32),
            pltpu.VMEM((2, NX * NZ, 4, CH), f32),
            pltpu.VMEM((NX * NZ, 4, CH), f32),
            pltpu.SemaphoreType.DMA((8,)),
            pltpu.SemaphoreType.DMA((2, 18)),
            pltpu.SemaphoreType.DMA((2, 5)),
            pltpu.SemaphoreType.DMA((2, 5)),
            pltpu.SemaphoreType.DMA((2, 2)),
            pltpu.SemaphoreType.DMA((2, 2)),
        ],
        compiler_params=pltpu.CompilerParams(
            collective_id=0, has_side_effects=True, vmem_limit_bytes=48 * 1024 * 1024
        ),
        cost_estimate=pl.CostEstimate(
            flops=4 * 1024 * 27 * CH * CH, bytes_accessed=2500000, transcendentals=800000
        ),
    )(*operands)


def solution(mesh):
    placed = (P("clip", "slab", None, None), P(), P(), P(), P(), P(), P(), P(), P(), P())
    return jax.shard_map(
        per_device,
        mesh=mesh,
        in_specs=placed,
        out_specs=P("clip", "slab", None, None),
        check_vma=False,
    )
```

time: 116 us -> 35.6 us (0.31)
  the two profiles are of different devices: /device:TPU:2 before, /device:TPU:1 now
where the time goes in v1:
time: 35.6 us; the launch traced here: 35.5 us
  Pallas kernels  34.8 us (98%)
  local copies, waits for them, and re-layouts  0.71 us (2%)
    pallas_call x1, Pallas kernels, per_device(): pl.pallas_call(kernel, out_shape=jax.ShapeDtypeStruct(x.shape, bf16), in_...  34.8 us

profile of v1, /device:TPU:1, one launch (start us, length us, event | category | flops | bytes accessed | tf_op | source)
XLA Modules:
  0.0 35.5 jit_solution(14992212699257498491)
XLA Ops:
  0.0 34.8 %shard_map.100 = bf16[2,4,128,128]{3,2,1,0:T(8,128)(2,1)S(1)} custom-call(bf16[2,4,128,128]{3,2,1,0:T(8,128)(2,1)} %x_hbm.1, s32[64]{0:T(128)} %ids_hbm.1, f32[1,128]{1,0:T(1,128)} %bitcast.6, f32[1,128]{1,0:T(1,128)} %bitcast.7, bf16[3,3,3,128,128]{4,3,2,1,0:T(8,128)(2,1)} %k1.1, f32[1,128]{1,0:T(1,128)} %bitcast.8, f32[1,128]{1,0:T(1,128)} %bitcast.9, ...), custom_call_target="tpu_custom_call" | custom-call | flops 1811939328 | bytes 2500000 | tf_op jit(solution)/shard_map/pallas_call | solution.py:277
  34.8 0.7 %copy.12 = bf16[2,4,128,128]{3,2,1,0:T(8,128)(2,1)} copy(bf16[2,4,128,128]{3,2,1,0:T(8,128)(2,1)S(1)} %shard_map.100) | data formatting | bytes 524288

commit v2 on v1

--- a/solution.py
+++ b/solution.py
@@ -18,19 +18,23 @@
     return min(dx, NX - dx) + min(dz, NZ - dz) + min(dy, NY - dy)
 
 
-NEAR = sorted(
-    [(dy, dc) for dy in range(NY) for dc in range(NC) if dy or dc],
-    key=lambda o: -hops(0, 0, o[0]),
-)
-FAR = sorted(
-    [(dx, dz) for dx in range(NX) for dz in range(NZ) if dx or dz],
-    key=lambda o: -hops(o[0], o[1], 0),
-)
+def offsets(nx, ny, nz, nc):
+    every = [
+        (dx, dy, dz, dc)
+        for dx in range(nx) for dy in range(ny) for dz in range(nz) for dc in range(nc)
+    ]
+    return sorted(every[1:], key=lambda o: -hops(o[0], o[2], o[1]))
+
+
+PLANE = offsets(NX, NY, 1, 1)
+LINE = offsets(1, 1, NZ, NC)
+EVERY = offsets(NX, NY, NZ, NC)
+AHEAD = sum(hops(o[0], o[2], o[1]) > 3 for o in EVERY)
 
 
 def kernel(
     x_hbm, ids_hbm, g1, s1, k1, b1, g2, s2, k2, b2, out_ref,
-    xbuf, hbuf, act, wts, pbuf, ids, vecs, near, far, mask,
+    xbuf, hbuf, act, wts, pbuf, ids, vecs, plane, line, every, line_mask, mask,
     load_sem, w_sem, halo_send, halo_recv, st_send, st_recv,
 ):
     clip = lax.axis_index("clip")
@@ -40,11 +44,12 @@
     cc = clip % NC
     clips = NX * NZ * NC
 
-    def near_dev(o):
-        return (clip - cc + (cc + o[1]) % NC, (y + o[0]) % NY)
-
-    def far_dev(o):
-        return (((cx + o[0]) % NX) * (NZ * NC) + ((cz + o[1]) % NZ) * NC + cc, y)
+    def device(o):
+        dx, dy, dz, dc = o
+        at = (cx + dx) % NX if dx else cx
+        at = at * NZ + ((cz + dz) % NZ if dz else cz)
+        at = at * NC + ((cc + dc) % NC if dc else cc)
+        return (at, (y + dy) % NY if dy else y)
 
     nxt, prv = (clip + 1) % clips, (clip + clips - 1) % clips
     up, down = (y + 1) % NY, (y + NY - 1) % NY
@@ -52,7 +57,7 @@
 
     barrier = pltpu.get_barrier_semaphore()
     n_signals = 0
-    for dev in [far_dev(o) for o in FAR] + halo_peers + [near_dev(o) for o in NEAR]:
+    for dev in [device(o) for o in PLANE + LINE] + halo_peers:
         pl.semaphore_signal(barrier, inc=1, device_id=dev, device_id_type=MESH)
         n_signals += 1
 
@@ -85,40 +90,32 @@
             q = q + jnp.sum(v * v, axis=0)
         return s, q
 
+    lane = lax.broadcasted_iota(jnp.int32, (1, CH), 1)
+    even = lane % 2 == 0
+
     def packed(s, q):
-        return jnp.concatenate(
-            [jnp.sum(s, axis=0, keepdims=True), jnp.sum(q, axis=0, keepdims=True)], axis=0
-        )
+        s = jnp.sum(s, axis=0, keepdims=True)
+        q = jnp.sum(q, axis=0, keepdims=True)
+        return jnp.where(even, s + pltpu.roll(s, CH - 1, 1), q + pltpu.roll(q, 1, 1))
 
     loads[0].wait()
     s, q = stats_of(
         xbuf[2 + f, 1 + r].astype(jnp.float32) for f in range(2) for r in range(4)
     )
-    me_near = y * NC + cc
-    me_far = cx * NZ + cz
-    near[0, me_near] = packed(s, q)
+    me_plane = cx * NY + y
+    me_line = cz * NC + cc
+    me = clip * NY + y
+    plane[me_plane] = packed(s, q)
 
     pl.semaphore_wait(barrier, n_signals)
 
-    def near_sends(ar):
+    def sends(offs, buf, at, n):
         cps = []
-        for o in NEAR:
+        for o in offs:
             cp = pltpu.make_async_remote_copy(
-                src_ref=near.at[ar, me_near], dst_ref=near.at[ar, me_near],
-                send_sem=st_send.at[ar, 0], recv_sem=st_recv.at[ar, 0],
-                device_id=near_dev(o), device_id_type=MESH,
-            )
-            cp.start()
-            cps.append(cp)
-        return cps
-
-    def far_sends(ar):
-        cps = []
-        for o in FAR:
-            cp = pltpu.make_async_remote_copy(
-                src_ref=far.at[ar, me_far], dst_ref=far.at[ar, me_far],
-                send_sem=st_send.at[ar, 1], recv_sem=st_recv.at[ar, 1],
-                device_id=far_dev(o), device_id_type=MESH,
+                src_ref=buf.at[at], dst_ref=buf.at[at],
+                send_sem=st_send.at[n], recv_sem=st_recv.at[n],
+                device_id=device(o), device_id_type=MESH,
             )
             cp.start()
             cps.append(cp)
@@ -145,22 +142,11 @@
             cps.append(cp)
         return cps
 
-    def wait_near(ar):
-        got = near.at[ar, pl.ds(0, len(NEAR))]
-        pltpu.make_async_copy(got, got, st_recv.at[ar, 0]).wait()
-
-    def wait_far(ar):
-        got = far.at[ar, pl.ds(0, len(FAR))]
-        pltpu.make_async_copy(got, got, st_recv.at[ar, 1]).wait()
-
-    def fold(ar):
-        for c in range(NC):
-            t = near[ar, c]
-            for k in range(1, NY):
-                t = t + near[ar, k * NC + c]
-            far[ar, me_far, 2 * c : 2 * c + 2, :] = t
-
-    near_1 = near_sends(0)
+    def arrived(buf, count, n):
+        got = buf.at[pl.ds(0, count)]
+        pltpu.make_async_copy(got, got, st_recv.at[n]).wait()
+
+    sent = sends(PLANE, plane, me_plane, 0)
     halo_1 = halo_sends(xbuf, 0)
 
     for cp in loads[1:]:
@@ -171,7 +157,9 @@
         for c in range(NC):
             m = jnp.where(ids[k * NC + c] == own_id, jnp.float32(1), jnp.float32(0))
             blocks = blocks + m
-            mask[k, 2 * c : 2 * c + 2, :] = jnp.full((2, CH), m, jnp.float32)
+            m = jnp.full((1, CH), m, jnp.float32)
+            mask[k * NC + c] = m
+            line_mask[(k % NZ) * NC + c, k // NZ : k // NZ + 1, :] = m
     prior_id = ids[jnp.maximum(clip - 1, 0)]
     same = jnp.where(prior_id == own_id, jnp.float32(1), jnp.float32(0))
     same = same * jnp.where(clip > 0, jnp.float32(1), jnp.float32(0))
@@ -184,20 +172,20 @@
             for dy in range(3):
                 wts[cv, dx, dy, 0:CH, CH : 2 * CH] = zero
                 wts[cv, dx, dy, 3 * CH : 4 * CH, 0:CH] = zero
-    lane = lax.broadcasted_iota(jnp.int32, (2, CH), 1)
-
-    def finish(ar, gain, shift):
-        acc = jnp.zeros((4, CH), jnp.float32)
-        for k in range(NX * NZ):
-            acc = acc + far[ar, k] * mask[k]
-        t = acc[0:2] + acc[2:4]
-        t = t + jnp.where(lane % 2 == 0, pltpu.roll(t, CH - 1, 1), pltpu.roll(t, 1, 1))
+
+    def finish(t, gain, shift):
         t = t + jnp.where(lane % 4 < 2, pltpu.roll(t, CH - 2, 1), pltpu.roll(t, 2, 1))
-        mean = t[0:1] * one_count
-        spread = t[1:2] * one_count - mean * mean
-        inverse = lax.rsqrt(spread + EPS)
+        t = t * one_count
+        mean = jnp.where(even, t, pltpu.roll(t, 1, 1))
+        square = jnp.where(even, pltpu.roll(t, CH - 1, 1), t)
+        inverse = lax.rsqrt(square - mean * mean + EPS)
         scale = inverse * gain
         return 0.5 * scale, 0.5 * (shift - mean * scale)
+
+    def tree(terms):
+        while len(terms) > 1:
+            terms = [sum(terms[k : k + 2][1:], terms[k]) for k in range(0, len(terms), 2)]
+        return terms[0]
 
     def activate(buf, scale, offset):
         for r in range(6):
@@ -225,15 +213,18 @@
         right = jnp.where(col == W - 1, 0.0, pltpu.roll(pbuf[(2, *at)], W - 1, 0))
         return (left + pbuf[(1, *at)]) + (right + bias)
 
-    wait_near(0)
-    fold(0)
-    far_1 = far_sends(0)
+    arrived(plane, len(PLANE), 0)
+    for k in range(NX):
+        line[me_line, k : k + 1, :] = tree([plane[k * NY + n] for n in range(NY)])
+    sent += sends(LINE, line, me_line, 1)
     for cp in w_loads:
         cp.wait()
     for cp in halo_1:
         cp.wait_recv()
-    wait_far(0)
-    scale, offset = finish(0, vecs[0], vecs[1])
+    arrived(line, len(LINE), 1)
+    t = tree([line[k] * line_mask[k] for k in range(NZ * NC)])
+    t = tree([t[k : k + 1] for k in range(NX)])
+    scale, offset = finish(t, vecs[0], vecs[1])
     activate(xbuf, scale, offset)
     convolve(0)
 
@@ -245,23 +236,26 @@
                 yield v.astype(jnp.float32)
 
     s, q = stats_of(hidden_rows())
-    near[1, me_near] = packed(s, q)
-    near_2 = near_sends(1)
+    every[me] = packed(s, q)
+    sent += sends(EVERY, every, me, 2)
     halo_2 = halo_sends(hbuf, 1)
-    wait_near(1)
-    fold(1)
-    far_2 = far_sends(1)
     for cp in halo_2:
         cp.wait_recv()
-    wait_far(1)
-    scale, offset = finish(1, vecs[3], vecs[4])
+    arrived(every, len(EVERY), 2)
+    t = tree(
+        [
+            tree([every[k * NY + n] for n in range(NY)]) * mask[k]
+            for k in range(NX * NZ * NC)
+        ]
+    )
+    scale, offset = finish(t, vecs[3], vecs[4])
     activate(hbuf, scale, offset)
     convolve(1)
     for f in range(2):
         for r in range(4):
             v = joined(f, r, vecs[5]) + xbuf[2 + f, 1 + r].astype(jnp.float32)
             out_ref[f, r] = v.astype(jnp.bfloat16)
-    for cp in near_1 + near_2 + far_1 + far_2 + halo_1 + halo_2:
+    for cp in sent + halo_1 + halo_2:
         cp.wait_send()
 
 
@@ -287,15 +281,17 @@
             pltpu.VMEM((3, 4 * W, 2 * CH), f32),
             pltpu.SMEM((64,), jnp.int32),
             pltpu.VMEM((6, 1, CH), f32),
-            pltpu.VMEM((2, NY * NC, 2, CH), f32),
-            pltpu.VMEM((2, NX * NZ, 4, CH), f32),
-            pltpu.VMEM((NX * NZ, 4, CH), f32),
+            pltpu.VMEM((NX * NY, 1, CH), f32),
+            pltpu.VMEM((NZ * NC, NX, CH), f32),
+            pltpu.VMEM((NX * NZ * NC * NY, 1, CH), f32),
+            pltpu.VMEM((NZ * NC, NX, CH), f32),
+            pltpu.VMEM((NX * NZ * NC, 1, CH), f32),
             pltpu.SemaphoreType.DMA((8,)),
             pltpu.SemaphoreType.DMA((2, 18)),
             pltpu.SemaphoreType.DMA((2, 5)),
             pltpu.SemaphoreType.DMA((2, 5)),
-            pltpu.SemaphoreType.DMA((2, 2)),
-            pltpu.SemaphoreType.DMA((2, 2)),
+            pltpu.SemaphoreType.DMA((3,)),
+            pltpu.SemaphoreType.DMA((3,)),
         ],
         compiler_params=pltpu.CompilerParams(
             collective_id=0, has_side_effects=True, vmem_limit_bytes=48 * 1024 * 1024

time: 35.6 us -> 34.6 us (0.972)
  the two profiles are of different devices: /device:TPU:1 before, /device:TPU:2 now
where the time goes in v2:
time: 34.6 us; the launch traced here: 34.4 us
  Pallas kernels  33.7 us (97%)
  local copies, waits for them, and re-layouts  0.71 us (2%)
    pallas_call x1, Pallas kernels, per_device(): pl.pallas_call(kernel, out_shape=jax.ShapeDtypeStruct(x.shape, bf16), in_...  33.7 us
    unnamed x1, local copies, waits for them, and re-layouts  0.71 us

profile of v2, /device:TPU:2, one launch (start us, length us, event | category | flops | bytes accessed | tf_op | source)
XLA Modules:
  0.0 34.4 jit_solution(6468078491678235467)
XLA Ops:
  0.0 33.7 %shard_map.100 = bf16[2,4,128,128]{3,2,1,0:T(8,128)(2,1)S(1)} custom-call(bf16[2,4,128,128]{3,2,1,0:T(8,128)(2,1)} %x_hbm.1, s32[64]{0:T(128)} %ids_hbm.1, f32[1,128]{1,0:T(1,128)} %bitcast.6, f32[1,128]{1,0:T(1,128)} %bitcast.7, bf16[3,3,3,128,128]{4,3,2,1,0:T(8,128)(2,1)} %k1.1, f32[1,128]{1,0:T(1,128)} %bitcast.8, f32[1,128]{1,0:T(1,128)} %bitcast.9, ...), custom_call_target="tpu_custom_call" | custom-call | flops 1811939328 | bytes 2500000 | tf_op jit(solution)/shard_map/pallas_call | solution.py:271
  33.7 0.7 %copy.12 = bf16[2,4,128,128]{3,2,1,0:T(8,128)(2,1)} copy(bf16[2,4,128,128]{3,2,1,0:T(8,128)(2,1)S(1)} %shard_map.100) | data formatting | bytes 524288

commit v3 on v2

--- a/solution.py
+++ b/solution.py
@@ -26,16 +26,17 @@
     return sorted(every[1:], key=lambda o: -hops(o[0], o[2], o[1]))
 
 
-PLANE = offsets(NX, NY, 1, 1)
-LINE = offsets(1, 1, NZ, NC)
+NEAR = offsets(NX, 1, 1, NC)
+FAR = offsets(1, NY, NZ, 1)
 EVERY = offsets(NX, NY, NZ, NC)
-AHEAD = sum(hops(o[0], o[2], o[1]) > 3 for o in EVERY)
+SIDE = [[o for o in EVERY if o[0] == dx] for dx in range(NX)]
+BEYOND = sorted({o[2:] for o in SIDE[2]}, key=lambda o: -hops(2, o[0], 0))
 
 
 def kernel(
     x_hbm, ids_hbm, g1, s1, k1, b1, g2, s2, k2, b2, out_ref,
-    xbuf, hbuf, act, wts, pbuf, ids, vecs, plane, line, every, line_mask, mask,
-    load_sem, w_sem, halo_send, halo_recv, st_send, st_recv,
+    xbuf, hbuf, act, wts, pbuf, ids, vecs, near, parts, far, every, far_mask, mask,
+    load_sem, w_sem, halo_send, halo_recv, st_send, st_recv, near_in, far_in,
 ):
     clip = lax.axis_index("clip")
     y = lax.axis_index("slab")
@@ -53,13 +54,35 @@
 
     nxt, prv = (clip + 1) % clips, (clip + clips - 1) % clips
     up, down = (y + 1) % NY, (y + NY - 1) % NY
-    halo_peers = [(nxt, y), (nxt, up), (nxt, down), (prv, y), (prv, up), (prv, down)]
 
     barrier = pltpu.get_barrier_semaphore()
-    n_signals = 0
-    for dev in [device(o) for o in PLANE + LINE] + halo_peers:
+
+    def greet(dev):
         pl.semaphore_signal(barrier, inc=1, device_id=dev, device_id_type=MESH)
-        n_signals += 1
+
+    def at(dx, dy, dz, core):
+        chip = ((cx + dx) % NX) * NZ + (cz + dz) % NZ
+        return (chip * NC + core, (y + dy) % NY)
+
+    for dx in range(1, NX):
+        greet(at(dx, 0, 0, 0))
+    for side in (up, down):
+        greet((clip - cc, side))
+
+    @pl.when(cc == 0)
+    def _():
+        for side in (y, up, down):
+            greet(((clip + clips - NC) % clips, side))
+        greet((clip + 1, y))
+
+    @pl.when(cc == 1)
+    def _():
+        greet((clip - 1, y))
+
+    for _, dy, dz, _ in FAR:
+        greet(at(0, dy, dz, 1))
+    heard_near = 2 * (NX - 1) + 1 + 4 + 3
+    heard_far = 2 * len(FAR) + 1
 
     loads = [pltpu.make_async_copy(x_hbm, xbuf.at[pl.ds(2, 2), pl.ds(1, 4)], load_sem.at[0])]
     loads.append(pltpu.make_async_copy(ids_hbm, ids, load_sem.at[1]))
@@ -98,22 +121,33 @@
         q = jnp.sum(q, axis=0, keepdims=True)
         return jnp.where(even, s + pltpu.roll(s, CH - 1, 1), q + pltpu.roll(q, 1, 1))
 
+    every[...] = jnp.zeros_like(every)
     loads[0].wait()
     s, q = stats_of(
         xbuf[2 + f, 1 + r].astype(jnp.float32) for f in range(2) for r in range(4)
     )
-    me_plane = cx * NY + y
-    me_line = cz * NC + cc
+    me_near = cx * NC + cc
+    me_far = y * NZ + cz
     me = clip * NY + y
-    plane[me_plane] = packed(s, q)
-
-    pl.semaphore_wait(barrier, n_signals)
+    near[me_near] = packed(s, q)
+
+    @pl.when(cc == 0)
+    def _():
+        pl.semaphore_wait(barrier, heard_near)
+        pl.semaphore_signal(near_in, inc=1, device_id=(clip + 1, y), device_id_type=MESH)
+
+    @pl.when(cc == 1)
+    def _():
+        pl.semaphore_wait(near_in, 1)
 
     def sends(offs, buf, at, n):
+        return copies([(o, buf.at[at], buf.at[at]) for o in offs], n)
+
+    def copies(plan, n):
         cps = []
-        for o in offs:
+        for o, src, dst in plan:
             cp = pltpu.make_async_remote_copy(
-                src_ref=buf.at[at], dst_ref=buf.at[at],
+                src_ref=src, dst_ref=dst,
                 send_sem=st_send.at[n], recv_sem=st_recv.at[n],
                 device_id=device(o), device_id_type=MESH,
             )
@@ -121,19 +155,9 @@
             cps.append(cp)
         return cps
 
-    def halo_sends(buf, n):
-        own = buf.at[pl.ds(2, 2), pl.ds(1, 4)]
-        first = buf.at[pl.ds(2, 2), 1]
-        last = buf.at[pl.ds(2, 2), 4]
-        plan = [
-            (own, buf.at[pl.ds(0, 2), pl.ds(1, 4)], (nxt, y)),
-            (last, buf.at[pl.ds(0, 2), 0], (nxt, up)),
-            (first, buf.at[pl.ds(0, 2), 5], (nxt, down)),
-            (last, buf.at[pl.ds(2, 2), 0], (clip, up)),
-            (first, buf.at[pl.ds(2, 2), 5], (clip, down)),
-        ]
+    def halo_sends(plan, n):
         cps = []
-        for m, (src, dst, dev) in enumerate(plan):
+        for m, (src, dst, dev) in plan:
             cp = pltpu.make_async_remote_copy(
                 src_ref=src, dst_ref=dst, send_sem=halo_send.at[n, m],
                 recv_sem=halo_recv.at[n, m], device_id=dev, device_id_type=MESH,
@@ -142,12 +166,44 @@
             cps.append(cp)
         return cps
 
+    frames = pl.ds(2, 2)
+    carried = pl.ds(0, 2)
+
+    def input_halo():
+        own, top_row, low_row = xbuf.at[frames, pl.ds(1, 4)], xbuf.at[frames, 1], xbuf.at[frames, 4]
+        plan = [
+            (own, xbuf.at[carried, pl.ds(1, 4)], (nxt, y)),
+            (low_row, xbuf.at[carried, 0], (nxt, up)),
+            (top_row, xbuf.at[carried, 5], (nxt, down)),
+            (low_row, xbuf.at[frames, 0], (clip, up)),
+            (top_row, xbuf.at[frames, 5], (clip, down)),
+        ]
+        return halo_sends(enumerate(plan), 0)
+
+    def hidden_halo(part):
+        rows = pl.ds(1 + 2 * part, 2)
+        edge, land, side = ((1, 5, down), (4, 0, up))[part]
+        plan = [
+            (hbuf.at[frames, rows], hbuf.at[carried, rows], (nxt, y)),
+            (hbuf.at[frames, edge], hbuf.at[carried, land], (nxt, side)),
+            (hbuf.at[frames, edge], hbuf.at[frames, land], (clip, side)),
+        ]
+        return halo_sends([(3 * part + m, copy) for m, copy in enumerate(plan)], 1)
+
+    def done(buf, count, sem):
+        got = buf.at[pl.ds(0, count)]
+        pltpu.make_async_copy(got, got, sem).wait()
+
     def arrived(buf, count, n):
-        got = buf.at[pl.ds(0, count)]
-        pltpu.make_async_copy(got, got, st_recv.at[n]).wait()
-
-    sent = sends(PLANE, plane, me_plane, 0)
-    halo_1 = halo_sends(xbuf, 0)
+        done(buf, count, st_recv.at[n])
+
+    def reached(dz, dc):
+        here = cz * NC + cc
+        there = ((cz + dz) % NZ) * NC + (cc + dc) % NC
+        return jnp.where(cx < 2, here - there, there - here) > 0
+
+    sent = sends(NEAR, near, me_near, 0)
+    halo_1 = input_halo()
 
     for cp in loads[1:]:
         cp.wait()
@@ -159,7 +215,12 @@
             blocks = blocks + m
             m = jnp.full((1, CH), m, jnp.float32)
             mask[k * NC + c] = m
-            line_mask[(k % NZ) * NC + c, k // NZ : k // NZ + 1, :] = m
+    column = [ids[(dx * NZ + cz) * NC + c] for dx in range(NX) for c in range(NC)]
+    for k in range(NZ):
+        target = ids[(cx * NZ + k) * NC + cc]
+        for n, member in enumerate(column):
+            m = jnp.where(member == target, jnp.float32(1), jnp.float32(0))
+            far_mask[k * NX * NC + n] = jnp.full((1, CH), m, jnp.float32)
     prior_id = ids[jnp.maximum(clip - 1, 0)]
     same = jnp.where(prior_id == own_id, jnp.float32(1), jnp.float32(0))
     same = same * jnp.where(clip > 0, jnp.float32(1), jnp.float32(0))
@@ -187,10 +248,10 @@
             terms = [sum(terms[k : k + 2][1:], terms[k]) for k in range(0, len(terms), 2)]
         return terms[0]
 
-    def activate(buf, scale, offset):
+    def activate(buf, scale, offset, frames):
         for r in range(6):
             row = top if r == 0 else bottom if r == 5 else None
-            for j in range(4):
+            for j in frames:
                 keep = row
                 if j < 2:
                     keep = same if row is None else same * row
@@ -199,11 +260,16 @@
                 v = h + h * jnp.tanh(h)
                 act[r * W : (r + 1) * W, j * CH : (j + 1) * CH] = v.astype(jnp.bfloat16)
 
-    def convolve(cv):
-        lhs = jnp.concatenate([act[d * W : (d + 4) * W, :] for d in range(3)], axis=1)
+    def convolve(cv, row, rows, frames, more=False):
+        out = slice(row * W, (row + rows) * W)
+        k = slice(frames[0] * CH, (frames[-1] + 1) * CH)
+        lhs = jnp.concatenate(
+            [act[(row + d) * W : (row + d + rows) * W, k] for d in range(3)], axis=1
+        )
         for dx in range(3):
-            rhs = wts[cv, dx].reshape(3 * 4 * CH, 2 * CH)
-            pbuf[dx] = jnp.dot(lhs, rhs, preferred_element_type=jnp.float32)
+            rhs = jnp.concatenate([wts[cv, dx, d, k, :] for d in range(3)], axis=0)
+            p = jnp.dot(lhs, rhs, preferred_element_type=jnp.float32)
+            pbuf[dx, out] = pbuf[dx, out] + p if more else p
 
     col = lax.broadcasted_iota(jnp.int32, (W, CH), 0)
 
@@ -213,35 +279,74 @@
         right = jnp.where(col == W - 1, 0.0, pltpu.roll(pbuf[(2, *at)], W - 1, 0))
         return (left + pbuf[(1, *at)]) + (right + bias)
 
-    arrived(plane, len(PLANE), 0)
-    for k in range(NX):
-        line[me_line, k : k + 1, :] = tree([plane[k * NY + n] for n in range(NY)])
-    sent += sends(LINE, line, me_line, 1)
+    @pl.when(cc == 1)
+    def _():
+        pl.semaphore_wait(barrier, heard_far)
+        pl.semaphore_signal(far_in, inc=1, device_id=(clip - 1, y), device_id_type=MESH)
+
+    @pl.when(cc == 0)
+    def _():
+        pl.semaphore_wait(far_in, 1)
+
+    arrived(near, len(NEAR), 0)
+    for k in range(NZ):
+        parts[k] = tree([near[n] * far_mask[k * NX * NC + n] for n in range(NX * NC)])
+    far[me_far] = parts[cz]
+    sent += copies([(o, parts.at[(cz + o[2]) % NZ], far.at[me_far]) for o in FAR], 1)
     for cp in w_loads:
         cp.wait()
     for cp in halo_1:
         cp.wait_recv()
-    arrived(line, len(LINE), 1)
-    t = tree([line[k] * line_mask[k] for k in range(NZ * NC)])
-    t = tree([t[k : k + 1] for k in range(NX)])
+    arrived(far, len(FAR), 1)
+    t = tree([far[k] for k in range(NY * NZ)])
     scale, offset = finish(t, vecs[0], vecs[1])
-    activate(xbuf, scale, offset)
-    convolve(0)
-
-    def hidden_rows():
+    activate(xbuf, scale, offset, range(4))
+
+    def hidden_rows(part):
         for f in range(2):
-            for r in range(4):
+            for r in range(2 * part, 2 * part + 2):
                 v = joined(f, r, vecs[2]).astype(jnp.bfloat16)
                 hbuf[2 + f, 1 + r] = v
                 yield v.astype(jnp.float32)
 
-    s, q = stats_of(hidden_rows())
+    convolve(0, 0, 2, range(4))
+    s, q = stats_of(hidden_rows(0))
+    convolve(0, 2, 2, range(4))
+    s2, q2 = stats_of(hidden_rows(1))
+    s, q = s + s2, q + q2
     every[me] = packed(s, q)
-    sent += sends(EVERY, every, me, 2)
-    halo_2 = halo_sends(hbuf, 1)
-    for cp in halo_2:
-        cp.wait_recv()
-    arrived(every, len(EVERY), 2)
+    for dz, dc in BEYOND:
+
+        @pl.when(reached(dz, dc))
+        def _():
+            sends([o for o in SIDE[2] if o[2:] == (dz, dc)], every, me, 5 + dz * NC + dc)
+
+    @pl.when(cx < NX - 1)
+    def _():
+        sends(SIDE[1], every, me, 3)
+
+    @pl.when(cx > 0)
+    def _():
+        sends(SIDE[3], every, me, 4)
+
+    sent += sends(SIDE[0], every, me, 2)
+    halo_2 = hidden_halo(0) + hidden_halo(1)
+    arrived(every, len(SIDE[0]), 2)
+
+    @pl.when(cx > 0)
+    def _():
+        arrived(every, len(SIDE[1]), 3)
+
+    @pl.when(cx < NX - 1)
+    def _():
+        arrived(every, len(SIDE[3]), 4)
+
+    for dz, dc in BEYOND:
+
+        @pl.when(reached(-dz, dc))
+        def _():
+            arrived(every, NY, 5 + dz * NC + dc)
+
     t = tree(
         [
             tree([every[k * NY + n] for n in range(NY)]) * mask[k]
@@ -249,14 +354,34 @@
         ]
     )
     scale, offset = finish(t, vecs[3], vecs[4])
-    activate(hbuf, scale, offset)
-    convolve(1)
+    for m in (2, 5):
+        halo_2[m].wait_recv()
+    activate(hbuf, scale, offset, range(2, 4))
+    convolve(1, 0, 4, range(2, 4))
+    for m in (0, 1, 3, 4):
+        halo_2[m].wait_recv()
+    activate(hbuf, scale, offset, range(2))
+    convolve(1, 0, 4, range(2), more=True)
     for f in range(2):
         for r in range(4):
             v = joined(f, r, vecs[5]) + xbuf[2 + f, 1 + r].astype(jnp.float32)
             out_ref[f, r] = v.astype(jnp.bfloat16)
     for cp in sent + halo_1 + halo_2:
         cp.wait_send()
+
+    @pl.when(cx < NX - 1)
+    def _():
+        done(every, len(SIDE[1]), st_send.at[3])
+
+    @pl.when(cx > 0)
+    def _():
+        done(every, len(SIDE[3]), st_send.at[4])
+
+    for dz, dc in BEYOND:
+
+        @pl.when(reached(dz, dc))
+        def _():
+            done(every, NY, st_send.at[5 + dz * NC + dc])
 
 
 def per_device(x, ids, g1, s1, k1, b1, g2, s2, k2, b2):
@@ -281,17 +406,20 @@
             pltpu.VMEM((3, 4 * W, 2 * CH), f32),
             pltpu.SMEM((64,), jnp.int32),
             pltpu.VMEM((6, 1, CH), f32),
-            pltpu.VMEM((NX * NY, 1, CH), f32),
-            pltpu.VMEM((NZ * NC, NX, CH), f32),
+            pltpu.VMEM((NX * NC, 1, CH), f32),
+            pltpu.VMEM((NZ, 1, CH), f32),
+            pltpu.VMEM((NY * NZ, 1, CH), f32),
             pltpu.VMEM((NX * NZ * NC * NY, 1, CH), f32),
-            pltpu.VMEM((NZ * NC, NX, CH), f32),
+            pltpu.VMEM((NZ * NX * NC, 1, CH), f32),
             pltpu.VMEM((NX * NZ * NC, 1, CH), f32),
             pltpu.SemaphoreType.DMA((8,)),
             pltpu.SemaphoreType.DMA((2, 18)),
-            pltpu.SemaphoreType.DMA((2, 5)),
-            pltpu.SemaphoreType.DMA((2, 5)),
-            pltpu.SemaphoreType.DMA((3,)),
-            pltpu.SemaphoreType.DMA((3,)),
+            pltpu.SemaphoreType.DMA((2, 7)),
+            pltpu.SemaphoreType.DMA((2, 7)),
+            pltpu.SemaphoreType.DMA((5 + NZ * NC,)),
+            pltpu.SemaphoreType.DMA((5 + NZ * NC,)),
+            pltpu.SemaphoreType.REGULAR,
+            pltpu.SemaphoreType.REGULAR,
         ],
         compiler_params=pltpu.CompilerParams(
             collective_id=0, has_side_effects=True, vmem_limit_bytes=48 * 1024 * 1024

time: 34.6 us -> 32.7 us (0.945)
  Pallas kernels: 33.7 us -> 31.6 us
    pallas_call x1, Pallas kernels: 33.7 us -> 31.6 us  [per_device(): pl.pallas_call(kernel, out_shape=jax.ShapeDtypeStruct(x.shape, bf16), in_...]
where the time goes in v3:
time: 32.7 us; the launch traced here: 32.3 us
  Pallas kernels  31.6 us (97%)
  local copies, waits for them, and re-layouts  0.71 us (2%)
    pallas_call x1, Pallas kernels, per_device(): pl.pallas_call(kernel, out_shape=jax.ShapeDtypeStruct(x.shape, bf16), in_...  31.6 us
    unnamed x1, local copies, waits for them, and re-layouts  0.71 us

profile of v3, /device:TPU:2, one launch (start us, length us, event | category | flops | bytes accessed | tf_op | source)
XLA Modules:
  0.0 32.3 jit_solution(16495956140916500558)
XLA Ops:
  0.0 31.6 %shard_map.100 = bf16[2,4,128,128]{3,2,1,0:T(8,128)(2,1)S(1)} custom-call(bf16[2,4,128,128]{3,2,1,0:T(8,128)(2,1)} %x_hbm.1, s32[64]{0:T(128)} %ids_hbm.1, f32[1,128]{1,0:T(1,128)} %bitcast.6, f32[1,128]{1,0:T(1,128)} %bitcast.7, bf16[3,3,3,128,128]{4,3,2,1,0:T(8,128)(2,1)} %k1.1, f32[1,128]{1,0:T(1,128)} %bitcast.8, f32[1,128]{1,0:T(1,128)} %bitcast.9, ...), custom_call_target="tpu_custom_call" | custom-call | flops 1811939328 | bytes 2500000 | tf_op jit(solution)/shard_map/pallas_call | solution.py:396
  31.6 0.7 %copy.12 = bf16[2,4,128,128]{3,2,1,0:T(8,128)(2,1)} copy(bf16[2,4,128,128]{3,2,1,0:T(8,128)(2,1)S(1)} %shard_map.100) | data formatting | bytes 524288

commit v4 on v3

--- a/solution.py
+++ b/solution.py
@@ -155,16 +155,18 @@
             cps.append(cp)
         return cps
 
-    def halo_sends(plan, n):
-        cps = []
-        for m, (src, dst, dev) in plan:
-            cp = pltpu.make_async_remote_copy(
+    def halo(plan, n):
+        return [
+            pltpu.make_async_remote_copy(
                 src_ref=src, dst_ref=dst, send_sem=halo_send.at[n, m],
                 recv_sem=halo_recv.at[n, m], device_id=dev, device_id_type=MESH,
             )
+            for m, (src, dst, dev) in plan
+        ]
+
+    def start(cps):
+        for cp in cps:
             cp.start()
-            cps.append(cp)
-        return cps
 
     frames = pl.ds(2, 2)
     carried = pl.ds(0, 2)
@@ -178,7 +180,7 @@
             (low_row, xbuf.at[frames, 0], (clip, up)),
             (top_row, xbuf.at[frames, 5], (clip, down)),
         ]
-        return halo_sends(enumerate(plan), 0)
+        return halo(enumerate(plan), 0)
 
     def hidden_halo(part):
         rows = pl.ds(1 + 2 * part, 2)
@@ -188,7 +190,7 @@
             (hbuf.at[frames, edge], hbuf.at[carried, land], (nxt, side)),
             (hbuf.at[frames, edge], hbuf.at[frames, land], (clip, side)),
         ]
-        return halo_sends([(3 * part + m, copy) for m, copy in enumerate(plan)], 1)
+        return halo([(3 * part + m, copy) for m, copy in enumerate(plan)], 1)
 
     def done(buf, count, sem):
         got = buf.at[pl.ds(0, count)]
@@ -204,6 +206,7 @@
 
     sent = sends(NEAR, near, me_near, 0)
     halo_1 = input_halo()
+    start(halo_1)
 
     for cp in loads[1:]:
         cp.wait()
@@ -311,26 +314,38 @@
 
     convolve(0, 0, 2, range(4))
     s, q = stats_of(hidden_rows(0))
+    ahead = jnp.logical_and(cz == NZ - 1, cc == 1)
+    halo_2 = hidden_halo(0) + hidden_halo(1)
+
+    @pl.when(ahead)
+    def _():
+        start(halo_2[:1])
+
     convolve(0, 2, 2, range(4))
     s2, q2 = stats_of(hidden_rows(1))
     s, q = s + s2, q + q2
     every[me] = packed(s, q)
+    @pl.when(cx > 0)
+    def _():
+        sends(SIDE[3], every, me, 4)
+
     for dz, dc in BEYOND:
 
         @pl.when(reached(dz, dc))
         def _():
             sends([o for o in SIDE[2] if o[2:] == (dz, dc)], every, me, 5 + dz * NC + dc)
 
+    sent += sends(SIDE[0], every, me, 2)
     @pl.when(cx < NX - 1)
     def _():
         sends(SIDE[1], every, me, 3)
 
-    @pl.when(cx > 0)
-    def _():
-        sends(SIDE[3], every, me, 4)
-
-    sent += sends(SIDE[0], every, me, 2)
-    halo_2 = hidden_halo(0) + hidden_halo(1)
+
+    @pl.when(jnp.logical_not(ahead))
+    def _():
+        start(halo_2[:1])
+
+    start(halo_2[1:])
     arrived(every, len(SIDE[0]), 2)
 
     @pl.when(cx > 0)

time: 32.7 us -> 32 us (0.979)
  Pallas kernels: 31.6 us -> 30.8 us
    pallas_call x1, Pallas kernels: 31.6 us -> 30.8 us  [per_device(): pl.pallas_call(kernel, out_shape=jax.ShapeDtypeStruct(x.shape, bf16), in_...]
where the time goes in v4:
time: 32 us; the launch traced here: 31.6 us
  Pallas kernels  30.8 us (96%)
  local copies, waits for them, and re-layouts  0.71 us (2%)
    pallas_call x1, Pallas kernels, per_device(): pl.pallas_call(kernel, out_shape=jax.ShapeDtypeStruct(x.shape, bf16), in_...  30.8 us
    unnamed x1, local copies, waits for them, and re-layouts  0.71 us

profile of v4, /device:TPU:2, one launch (start us, length us, event | category | flops | bytes accessed | tf_op | source)
XLA Modules:
  0.0 31.6 jit_solution(171746192529670040)
XLA Ops:
  0.0 30.8 %shard_map.100 = bf16[2,4,128,128]{3,2,1,0:T(8,128)(2,1)S(1)} custom-call(bf16[2,4,128,128]{3,2,1,0:T(8,128)(2,1)} %x_hbm.1, s32[64]{0:T(128)} %ids_hbm.1, f32[1,128]{1,0:T(1,128)} %bitcast.6, f32[1,128]{1,0:T(1,128)} %bitcast.7, bf16[3,3,3,128,128]{4,3,2,1,0:T(8,128)(2,1)} %k1.1, f32[1,128]{1,0:T(1,128)} %bitcast.8, f32[1,128]{1,0:T(1,128)} %bitcast.9, ...), custom_call_target="tpu_custom_call" | custom-call | flops 1811939328 | bytes 2500000 | tf_op jit(solution)/shard_map/pallas_call | solution.py:411
  30.9 0.7 %copy.12 = bf16[2,4,128,128]{3,2,1,0:T(8,128)(2,1)} copy(bf16[2,4,128,128]{3,2,1,0:T(8,128)(2,1)S(1)} %shard_map.100) | data formatting | bytes 524288

commit v5 on v4

--- a/solution.py
+++ b/solution.py
@@ -182,15 +182,17 @@
         ]
         return halo(enumerate(plan), 0)
 
-    def hidden_halo(part):
-        rows = pl.ds(1 + 2 * part, 2)
-        edge, land, side = ((1, 5, down), (4, 0, up))[part]
+    def hidden_halo():
         plan = [
-            (hbuf.at[frames, rows], hbuf.at[carried, rows], (nxt, y)),
-            (hbuf.at[frames, edge], hbuf.at[carried, land], (nxt, side)),
-            (hbuf.at[frames, edge], hbuf.at[frames, land], (clip, side)),
+            (hbuf.at[frames, 1], hbuf.at[carried, 1], (nxt, y)),
+            (hbuf.at[frames, 4], hbuf.at[carried, 4], (nxt, y)),
+            (hbuf.at[frames, 1], hbuf.at[frames, 5], (clip, down)),
+            (hbuf.at[frames, 4], hbuf.at[frames, 0], (clip, up)),
+            (hbuf.at[frames, pl.ds(2, 2)], hbuf.at[carried, pl.ds(2, 2)], (nxt, y)),
+            (hbuf.at[carried, 1], hbuf.at[carried, 5], (clip, down)),
+            (hbuf.at[carried, 4], hbuf.at[carried, 0], (clip, up)),
         ]
-        return halo([(3 * part + m, copy) for m, copy in enumerate(plan)], 1)
+        return halo(enumerate(plan), 1)
 
     def done(buf, count, sem):
         got = buf.at[pl.ds(0, count)]
@@ -263,16 +265,22 @@
                 v = h + h * jnp.tanh(h)
                 act[r * W : (r + 1) * W, j * CH : (j + 1) * CH] = v.astype(jnp.bfloat16)
 
-    def convolve(cv, row, rows, frames, more=False):
-        out = slice(row * W, (row + rows) * W)
+    def convolve(cv, rows, frames, more=False):
         k = slice(frames[0] * CH, (frames[-1] + 1) * CH)
         lhs = jnp.concatenate(
-            [act[(row + d) * W : (row + d + rows) * W, k] for d in range(3)], axis=1
+            [
+                jnp.concatenate([act[(r + d) * W : (r + d + 1) * W, k] for r in rows], axis=0)
+                for d in range(3)
+            ],
+            axis=1,
         )
         for dx in range(3):
             rhs = jnp.concatenate([wts[cv, dx, d, k, :] for d in range(3)], axis=0)
             p = jnp.dot(lhs, rhs, preferred_element_type=jnp.float32)
-            pbuf[dx, out] = pbuf[dx, out] + p if more else p
+            for n, r in enumerate(rows):
+                out = slice(r * W, (r + 1) * W)
+                part = p[n * W : (n + 1) * W]
+                pbuf[dx, out] = pbuf[dx, out] + part if more else part
 
     col = lax.broadcasted_iota(jnp.int32, (W, CH), 0)
 
@@ -305,24 +313,19 @@
     scale, offset = finish(t, vecs[0], vecs[1])
     activate(xbuf, scale, offset, range(4))
 
-    def hidden_rows(part):
+    def hidden_rows(rows):
         for f in range(2):
-            for r in range(2 * part, 2 * part + 2):
+            for r in rows:
                 v = joined(f, r, vecs[2]).astype(jnp.bfloat16)
                 hbuf[2 + f, 1 + r] = v
                 yield v.astype(jnp.float32)
 
-    convolve(0, 0, 2, range(4))
-    s, q = stats_of(hidden_rows(0))
-    ahead = jnp.logical_and(cz == NZ - 1, cc == 1)
-    halo_2 = hidden_halo(0) + hidden_halo(1)
-
-    @pl.when(ahead)
-    def _():
-        start(halo_2[:1])
-
-    convolve(0, 2, 2, range(4))
-    s2, q2 = stats_of(hidden_rows(1))
+    convolve(0, (0, 3), range(4))
+    s, q = stats_of(hidden_rows((0, 3)))
+    halo_2 = hidden_halo()
+    start(halo_2[:2])
+    convolve(0, (1, 2), range(4))
+    s2, q2 = stats_of(hidden_rows((1, 2)))
     s, q = s + s2, q + q2
     every[me] = packed(s, q)
     @pl.when(cx > 0)
@@ -341,11 +344,10 @@
         sends(SIDE[1], every, me, 3)
 
 
-    @pl.when(jnp.logical_not(ahead))
-    def _():
-        start(halo_2[:1])
-
-    start(halo_2[1:])
+    start(halo_2[4:5] + halo_2[2:4])
+    for m in range(2):
+        halo_2[m].wait_recv()
+        halo_2[5 + m].start()
     arrived(every, len(SIDE[0]), 2)
 
     @pl.when(cx > 0)
@@ -369,14 +371,14 @@
         ]
     )
     scale, offset = finish(t, vecs[3], vecs[4])
-    for m in (2, 5):
+    for m in (2, 3):
         halo_2[m].wait_recv()
     activate(hbuf, scale, offset, range(2, 4))
-    convolve(1, 0, 4, range(2, 4))
-    for m in (0, 1, 3, 4):
+    convolve(1, range(4), range(2, 4))
+    for m in (4, 5, 6):
         halo_2[m].wait_recv()
     activate(hbuf, scale, offset, range(2))
-    convolve(1, 0, 4, range(2), more=True)
+    convolve(1, range(4), range(2), more=True)
     for f in range(2):
         for r in range(4):
             v = joined(f, r, vecs[5]) + xbuf[2 + f, 1 + r].astype(jnp.float32)

time: 32 us -> 30.9 us (0.966)
  Pallas kernels: 30.8 us -> 29.8 us
    pallas_call x1, Pallas kernels: 30.8 us -> 29.8 us  [per_device(): pl.pallas_call(kernel, out_shape=jax.ShapeDtypeStruct(x.shape, bf16), in_...]
where the time goes in v5:
time: 30.9 us; the launch traced here: 30.5 us
  Pallas kernels  29.8 us (96%)
  local copies, waits for them, and re-layouts  0.71 us (2%)
    pallas_call x1, Pallas kernels, per_device(): pl.pallas_call(kernel, out_shape=jax.ShapeDtypeStruct(x.shape, bf16), in_...  29.8 us
    unnamed x1, local copies, waits for them, and re-layouts  0.71 us

profile of v5, /device:TPU:2, one launch (start us, length us, event | category | flops | bytes accessed | tf_op | source)
XLA Modules:
  0.0 30.5 jit_solution(3508036504288169504)
XLA Ops:
  0.0 29.8 %shard_map.100 = bf16[2,4,128,128]{3,2,1,0:T(8,128)(2,1)S(1)} custom-call(bf16[2,4,128,128]{3,2,1,0:T(8,128)(2,1)} %x_hbm.1, s32[64]{0:T(128)} %ids_hbm.1, f32[1,128]{1,0:T(1,128)} %bitcast.6, f32[1,128]{1,0:T(1,128)} %bitcast.7, bf16[3,3,3,128,128]{4,3,2,1,0:T(8,128)(2,1)} %k1.1, f32[1,128]{1,0:T(1,128)} %bitcast.8, f32[1,128]{1,0:T(1,128)} %bitcast.9, ...), custom_call_target="tpu_custom_call" | custom-call | flops 1811939328 | bytes 2500000 | tf_op jit(solution)/shard_map/pallas_call | solution.py:413
  29.8 0.7 %copy.12 = bf16[2,4,128,128]{3,2,1,0:T(8,128)(2,1)} copy(bf16[2,4,128,128]{3,2,1,0:T(8,128)(2,1)S(1)} %shard_map.100) | data formatting | bytes 524288

commit v6 on v5

--- a/solution.py
+++ b/solution.py
@@ -371,14 +371,10 @@
         ]
     )
     scale, offset = finish(t, vecs[3], vecs[4])
-    for m in (2, 3):
-        halo_2[m].wait_recv()
-    activate(hbuf, scale, offset, range(2, 4))
-    convolve(1, range(4), range(2, 4))
-    for m in (4, 5, 6):
-        halo_2[m].wait_recv()
-    activate(hbuf, scale, offset, range(2))
-    convolve(1, range(4), range(2), more=True)
+    for cp in halo_2[2:]:
+        cp.wait_recv()
+    activate(hbuf, scale, offset, range(4))
+    convolve(1, range(4), range(4))
     for f in range(2):
         for r in range(4):
             v = joined(f, r, vecs[5]) + xbuf[2 + f, 1 + r].astype(jnp.float32)

time: 30.9 us -> 31 us (level)
  no operation moved by 1% of the time
where the time goes in v6:
time: 31 us; the launch traced here: 30.6 us
  Pallas kernels  29.9 us (96%)
  local copies, waits for them, and re-layouts  0.71 us (2%)
    pallas_call x1, Pallas kernels, per_device(): pl.pallas_call(kernel, out_shape=jax.ShapeDtypeStruct(x.shape, bf16), in_...  29.9 us
    unnamed x1, local copies, waits for them, and re-layouts  0.71 us

profile of v6, /device:TPU:2, one launch (start us, length us, event | category | flops | bytes accessed | tf_op | source)
XLA Modules:
  0.0 30.6 jit_solution(3804830411055781182)
XLA Ops:
  0.0 29.9 %shard_map.100 = bf16[2,4,128,128]{3,2,1,0:T(8,128)(2,1)S(1)} custom-call(bf16[2,4,128,128]{3,2,1,0:T(8,128)(2,1)} %x_hbm.1, s32[64]{0:T(128)} %ids_hbm.1, f32[1,128]{1,0:T(1,128)} %bitcast.6, f32[1,128]{1,0:T(1,128)} %bitcast.7, bf16[3,3,3,128,128]{4,3,2,1,0:T(8,128)(2,1)} %k1.1, f32[1,128]{1,0:T(1,128)} %bitcast.8, f32[1,128]{1,0:T(1,128)} %bitcast.9, ...), custom_call_target="tpu_custom_call" | custom-call | flops 1811939328 | bytes 2500000 | tf_op jit(solution)/shard_map/pallas_call | solution.py:409
  29.9 0.7 %copy.12 = bf16[2,4,128,128]{3,2,1,0:T(8,128)(2,1)} copy(bf16[2,4,128,128]{3,2,1,0:T(8,128)(2,1)S(1)} %shard_map.100) | data formatting | bytes 524288
